TPU v7x, 128 devices: a whole 4x4x4 slice. The times are simulated.
128 devices in a mesh: dp: 32 (over x, y_lo, z), code: 4 (over y_hi, core).
Axes of the slice: x: 4, y: 4 (y_hi: 2, y_lo: 2; y = y_hi * 2 + y_lo), z: 4, core: 2. Of those that a mesh axis runs over, the one named last changes fastest.
Arguments:
- grads: bfloat16 [32, 4, 512, 16384], P('dp', 'code'), may hold values from -1.59375 to 1.59375
- master: float32 [4, 512, 16384], P('code', 'dp'), may hold values from -6 to 6
- moment_one: float32 [4, 512, 16384], P('code', 'dp'), may hold values from -3 to 3
- moment_two: float32 [4, 512, 16384], P('code', 'dp'), may hold values from 0.05 to 1
- generator: float32 [4, 16], replicated, may hold values from 0.5 to 2
- member_slot: int32 [32, 4], P('dp', 'code'), may hold values from 0 to 15, as said below
- holder: int32 [32, 4], replicated, may hold values from 0 to 15, as said below
Outputs:
- updated: float32 [4, 512, 16384], P('code', 'dp')
- new_one: float32 [4, 512, 16384], P('code', 'dp')
- new_two: float32 [4, 512, 16384], P('code', 'dp')
- parity: float32 [4, 128, 16384], P('code', 'dp')
Inputs may be any that keep to these rules, and one draw needn't show every extreme that they name: `member_slot`: within each coding group (the devices whose dp index has the same remainder modulo 8), the 16 devices have 16 different slots. `holder`: within each coding group, the 16 devices hold 16 different blocks.
All inputs are finite; a program needn't handle non-finite values.
Results may differ from a plain program's by a relative error of at most 0.0003.
Values sent between devices are 32-bit elements; how exact they have to be, the bound alone decides.
A program may use at most 128 MiB of HBM per device.

v0:
```python
import jax
import jax.numpy as jnp
from jax import lax
from jax.sharding import PartitionSpec as P

beta_one = 0.9
beta_two = 0.999
learn_rate = 0.05
decay_rate = 0.1
epsilon = 1e-08
correct_one = 1.0 - 0.9**10
correct_two = 1.0 - 0.999**10


def swapped(value, axis, apart):
    mask = 2**apart
    pairs = [(source, source ^ mask) for source in range(lax.axis_size(axis))]
    return lax.ppermute(value, axis, pairs)


def code_total(values):
    return lax.psum_scatter(values, "code", scatter_dimension=0, tiled=True)


def pair_total(values, own_index, top_bit):
    for bit_number in (top_bit, top_bit - 1):
        half = values.shape[1] // 2
        lower = values[:, :half]
        upper = values[:, half:]
        upper_side = own_index >> bit_number & 1 == 1
        keeping = jnp.where(upper_side, upper, lower)
        sending = jnp.where(upper_side, lower, upper)
        values = keeping + swapped(sending, "dp", bit_number)
    return values


def shards(grads, master, moment_one, moment_two, generator, member_slot, holder):
    dp_size = lax.axis_size("dp")
    stride = dp_size // 4
    top_bit = dp_size.bit_length() - 2
    own_index = lax.axis_index("dp")
    group_index = own_index % stride
    rows_owned = master.shape[1]
    width = master.shape[2]
    quarter = rows_owned // 4
    slot_value = member_slot[0, 0]
    table = holder.reshape(4, stride, holder.shape[1])
    members = jnp.transpose(
        lax.dynamic_slice_in_dim(table, group_index, 1, 1).reshape(4, 4)
    ).reshape(16)
    column = jnp.sum(
        generator * (jnp.arange(16) == slot_value)[None, :].astype(jnp.float32), axis=1
    )
    parity_of = members // 4
    part_of = members % 4
    coefficients = jnp.sum(
        column[None, :] * (parity_of[:, None] == jnp.arange(4)[None, :]).astype(jnp.float32), axis=1
    )
    selector = coefficients[:, None] * (part_of[:, None] == jnp.arange(4)[None, :]).astype(
        jnp.float32
    )
    pieces = 1
    block_width = width // pieces
    grad_block = grads.astype(jnp.float32)
    summed = lax.psum_scatter(grad_block, "dp", scatter_dimension=2, tiled=True)[0, 0]
    weights = master[0, :, 0:block_width]
    new_one = beta_one * moment_one[0, :, 0:block_width] + (1.0 - beta_one) * summed
    new_two = beta_two * moment_two[0, :, 0:block_width] + (1.0 - beta_two) * summed * summed
    direction = new_one / correct_one / (jnp.sqrt(new_two / correct_two) + epsilon)
    updated = weights - learn_rate * (direction + decay_rate * weights)
    quarters = updated.reshape(4, quarter, block_width)
    terms = jnp.einsum("qk,krd->qrd", selector, quarters, precision=lax.Precision.HIGHEST)
    terms = terms.reshape(4, 4, quarter, block_width)
    reduced = pair_total(code_total(terms), own_index, top_bit)
    outs_parity = reduced.reshape(quarter, block_width)
    updated_all = updated[None]
    one_all = new_one[None]
    two_all = new_two[None]
    parity_all = outs_parity[None]
    return (updated_all, one_all, two_all, parity_all)


def solution(mesh):
    return jax.shard_map(
        shards,
        mesh=mesh,
        in_specs=(
            P("dp", "code", None, None),
            P("code", "dp", None),
            P("code", "dp", None),
            P("code", "dp", None),
            P(),
            P("dp", "code"),
            P(),
        ),
        out_specs=(
            P("code", "dp", None),
            P("code", "dp", None),
            P("code", "dp", None),
            P("code", "dp", None),
        ),
        check_vma=False,
    )
```

profile of v0, /device:TPU:0, one launch (start us, length us, event | category | flops | bytes accessed | tf_op | source)
XLA Modules:
  0.0 530.1 jit_solution(5980673272426543914)
XLA Ops:
  7.2 0.0 reduce-scatter.2.cloned.1.call-start
  7.2 18.2 %convert_element_type.13 = f32[1,1,512,16384]{3,2,1,0:T(8,128)} convert(bf16[1,1,512,16384]{3,2,1,0:T(8,128)(2,1)} %param.7) | non-fusion elementwise | flops 8388608 | bytes 50331648 | tf_op jit(solution)/shard_map/convert_element_type | solution.py:64
  25.4 0.0 copy-start.3
  25.4 0.0 copy-start.4
  25.4 0.0 copy-start.1
  25.4 0.0 copy-start.2
  25.4 0.0 reduce-scatter.2.cloned.1.call-update
  25.5 0.0 all-reduce.3.cloned.1.call-start
  25.5 0.6 copy-done.3
  26.1 0.1 reshape.141
  26.2 0.1 constant_dynamic-slice_fusion
  26.3 0.1 copy.27
  26.4 0.1 copy.21
  27.1 0.1 reshape.143
  27.2 0.0 copy-done.4
  27.2 0.1 multiply_reduce_fusion
  27.3 0.1 select_reduce_fusion
  27.4 0.1 mul.120
  27.5 0.1 copy.22
  27.6 365.2 %reduce-scatter.2.cloned.1.call-done = f32[1,1,16,16384]{3,2,1,0:T(8,128)} async-done(((f32[1,1,512,16384]{3,2,1,0:T(8,128)}), f32[1,1,16,16384]{3,2,1,0:T(8,128)}) %reduce-scatter.2.cloned.1.call-update) | async-done | bytes 1048592 | tf_op jit(solution)/shard_map/reduce_scatter | solution.py:65
  392.8 0.0 copy-done.1
  392.8 0.0 copy-done.2
  392.8 3.6 multiply_subtract_fusion
  396.4 0.0 copy-start
  396.4 0.3 sub.14
  396.7 0.0 copy-start.5
  396.7 6.5 %fusion.1 = f32[4,4,4,16384]{3,1,2,0:T(4,128)} fusion(f32[4,4,16384]{2,1,0:T(4,128)S(1)} %sub.14, f32[4,4]{1,0:T(4,128)S(1)} %mul.120, s32[4,4]{1,0:T(4,128)S(1)} %copy.22), kind=kOutput, calls=%fused_computation.2 | convolution fusion | flops 50331776 | bytes 5243008 | tf_op jit(solution)/shard_map/qk,krd->qrd/dot_general | solution.py:72
  403.2 0.0 all-reduce.3.cloned.1.call-update
  403.2 0.0 copy-done
  403.2 0.0 copy-done.5
  403.3 0.6 dynamic-slice
  403.8 89.0 %all-reduce.3.cloned.1.call-done = f32[4,4,4,16384]{3,1,2,0:T(4,128)} async-done(((f32[4,4,4,16384]{3,1,2,0:T(4,128)}), f32[4,4,4,16384]{3,1,2,0:T(4,128)}) %all-reduce.3.cloned.1.call-update) | async-done | bytes 4194320
  492.8 2.5 broadcast_select_fusion
  495.3 3.1 collective-permute-start
  498.4 12.7 %collective-permute-done = f32[1,2,4,16384]{3,1,2,0:T(2,128)S(1)} collective-permute-done((f32[1,2,4,16384]{3,1,2,0:T(2,128)S(1)}, f32[1,2,4,16384]{3,1,2,0:T(2,128)S(1)}, u32[]{:S(2)}, u32[]{:S(2)}) %collective-permute-start) | collective-permute-done | bytes 524320 | tf_op jit(solution)/shard_map/ppermute | solution.py:18
  511.1 2.6 select_add_fusion
  513.7 0.3 broadcast_select_fusion.1
  514.0 1.5 collective-permute-start.1
  515.6 6.4 %collective-permute-done.1 = f32[1,1,4,16384]{3,1,2,0:T(1,128)S(1)} collective-permute-done((f32[1,1,4,16384]{3,1,2,0:T(1,128)S(1)}, f32[1,1,4,16384]{3,1,2,0:T(1,128)S(1)}, u32[]{:S(2)}, u32[]{:S(2)}) %collective-permute-start.1) | collective-permute-done | bytes 262176 | tf_op jit(solution)/shard_map/ppermute | solution.py:18
  522.0 0.4 fusion.6
  522.4 0.9 copy.25
  (3 shorter events, 0.0 us)
Async XLA Ops:
  7.2 385.6 %reduce-scatter.2.cloned.1.call-start = ((), (), s32[]{:S(2)}) async-start(), calls=%async_computation.1 | async-start | bytes 34603008 | tf_op jit(solution)/shard_map/reduce_scatter | solution.py:65
  25.4 0.7 copy-start.3
  25.4 1.8 copy-start.4
  25.4 367.4 %copy-start.1 = (f32[1,16,16384]{2,1,0:T(8,128)S(1)}, f32[1,16,16384]{2,1,0:T(8,128)}, u32[]{:S(2)}) copy-start(f32[1,16,16384]{2,1,0:T(8,128)} %param.8) | copy-start | bytes 3145732
  25.4 367.4 %copy-start.2 = (f32[1,16,16384]{2,1,0:T(8,128)S(1)}, f32[1,16,16384]{2,1,0:T(8,128)}, u32[]{:S(2)}) copy-start(f32[1,16,16384]{2,1,0:T(8,128)} %param.9) | copy-start | bytes 3145732
  25.5 467.3 %all-reduce.3.cloned.1.call-start = ((), (), s32[]{:S(2)}) async-start(), calls=%async_computation.2 | async-start | bytes 8388608
  396.4 6.8 %copy-start = (f32[1,16,16384]{2,1,0:T(8,128)}, f32[1,16,16384]{2,1,0:T(8,128)S(1)}, u32[]{:S(2)}) copy-start(f32[1,16,16384]{2,1,0:T(8,128)S(1)} %get-tuple-element.16) | copy-start | bytes 3145732
  396.7 6.5 %copy-start.5 = (u32[128]{0:T(128)S(1)}, u32[128]{0:T(128)}, u32[]{:S(2)}) copy-start(u32[128]{0:T(128)} %constant.78) | copy-start | bytes 1540
  495.3 15.8 %collective-permute-start = (f32[1,2,4,16384]{3,1,2,0:T(2,128)S(1)}, f32[1,2,4,16384]{3,1,2,0:T(2,128)S(1)}, u32[]{:S(2)}, u32[]{:S(2)}) collective-permute-start(f32[1,2,4,16384]{3,1,2,0:T(2,128)S(1)} %broadcast_select_fusion), channel_id=1, source_target_pairs={{0,64},{4,68},{8,72},{12,76},{16,80},{20,84},{24,88},{28,92},{32,9... | collective-permute-start | bytes 1572872 | tf_op jit(solution)/shard_map/ppermute | solution.py:18
  514.0 7.9 %collective-permute-start.1 = (f32[1,1,4,16384]{3,1,2,0:T(1,128)S(1)}, f32[1,1,4,16384]{3,1,2,0:T(1,128)S(1)}, u32[]{:S(2)}, u32[]{:S(2)}) collective-permute-start(f32[1,1,4,16384]{3,1,2,0:T(1,128)S(1)} %broadcast_select_fusion.1), channel_id=1, source_target_pairs={{0,32},{4,36},{8,40},{12,44},{16,48},{20,52},{24,56},{28,60},{32,0... | collective-permute-start | bytes 786440 | tf_op jit(solution)/shard_map/ppermute | solution.py:18
Sparse Core Ops, SparseCore 0:
  25.6 367.1 reduce-scatter.1
  403.3 89.4 all-reduce.2
where the time goes:
time: 530 us
  waiting for transfers between devices  473 us (89%)
  other arithmetic  27.9 us (5%)
  between operations  14.8 us (3%)
  matrix products  6.47 us (1%)
    reduce_scatter x1, waiting for transfers between devices, shards(): lax.psum_scatter(grad_block, 'dp', scatter_dimension=2, tiled=True)[0, 0]  365 us
    unnamed x3, waiting for transfers between devices  89 us
    ppermute x2, waiting for transfers between devices, swapped(): return lax.ppermute(value, axis, pairs)  19.1 us
    convert_element_type x1, other arithmetic, shards(): grad_block = grads.astype(jnp.float32)  18.2 us
  transfers between devices with their start and end apart: 4, of which 4 were waited for; matrix products, arithmetic and copies ran while one was open for 0% of the time, Pallas kernels for 0%

commit v1 on v0

v1 whole, which is shorter than its diff:
```python
import functools

import jax
import jax.numpy as jnp
from jax import lax
from jax.experimental import pallas as pl
from jax.experimental.pallas import tpu as pltpu
from jax.sharding import PartitionSpec as P

MESH = pl.DeviceIdType.MESH

beta_one = 0.9
beta_two = 0.999
learn_rate = 0.05
decay_rate = 0.1
epsilon = 1e-08
correct_one = 1.0 - 0.9**10
correct_two = 1.0 - 0.999**10

D = 16384
X, Z, Y = range(3)
XP, XM, X2, ZP, ZM, Z2, YN, YH, CORE, XPH, XMH, X2H = range(12)
AXES = {X: ((XP, XM, X2), (ZP, ZM, Z2)), Z: ((ZP, ZM, Z2), (XP, XM, X2)), Y: ((ZP, ZM, Z2), (XP, XM, X2))}
WIDE = {X: 384, Z: 256, Y: 384}
WIDE_STEPS = 14
NARROW = {X: 128, Z: 128, Y: 256}
NARROW_STEPS = 4
WIDE_COLS, NARROW_COLS = sum(WIDE.values()), sum(NARROW.values())
GRAD_SLOTS = 5
SLOTS = 3
PLACE = {(2, 0): 0, (1, 1): 1, (2, 1): 2, (3, 0): 3, (1, 0): 4, (3, 1): 5, (0, 0): 6, (0, 1): 7}

assert WIDE_COLS * WIDE_STEPS + NARROW_COLS * NARROW_STEPS == D


class Scratch:
    def __init__(self, pool, spec):
        self.spec, self.ref = spec, None
        pool.append(self)


class Copy:
    def __init__(self, pool, to, src, dst, slots, steps):
        self.to, self.src, self.dst, self.slots = to, src, dst, slots
        self.send = Scratch(pool, pltpu.SemaphoreType.DMA((slots,)))
        self.recv = Scratch(pool, pltpu.SemaphoreType.DMA((steps,)))

    def at(self, c, where):
        slot = lax.rem(c, self.slots)
        return pltpu.make_async_remote_copy(
            src_ref=self.src(slot, c),
            dst_ref=self.dst(c),
            send_sem=self.send.ref.at[slot],
            recv_sem=self.recv.ref.at[c],
            device_id=where[self.to],
            device_id_type=MESH,
        )


class Ring:
    def __init__(self, pool, axis, steps, rows, cols, staged):
        self.came = [Scratch(pool, pltpu.VMEM((steps, 2, rows, cols), jnp.float32)) for _ in range(2)]
        self.passed = Scratch(pool, pltpu.VMEM((steps, 2, rows, cols), jnp.float32))
        self.copies, self.on = [], []
        if staged:
            self.staged = [Scratch(pool, pltpu.VMEM((SLOTS, 2, rows, cols), jnp.float32)) for _ in range(2)]
        else:
            self.acc = Scratch(pool, pltpu.VMEM((SLOTS, 8, rows, cols), jnp.float32))
        for way in range(2):

            def first(slot, c, way=way):
                return self.staged[way].ref.at[slot] if staged else self.acc.ref.at[slot, pl.ds(2 * way, 2)]

            def landed(c, way=way):
                return self.came[way].ref.at[c]

            def second(slot, c, way=way):
                return self.came[way].ref.at[c, 0]

            def last(c, way=way):
                return self.passed.ref.at[c, way]

            self.copies.append(Copy(pool, axis[way], first, landed, SLOTS, steps))
            self.on.append(Copy(pool, axis[way], second, last, SLOTS, steps))


class Direct:
    def __init__(self, pool, axis, steps, rows, cols):
        self.acc = Scratch(pool, pltpu.VMEM((steps, 4, rows, cols), jnp.float32))
        self.came = Scratch(pool, pltpu.VMEM((steps, 3, rows, cols), jnp.float32))
        self.copies = []
        for k, to in ((1, axis[0]), (2, axis[2]), (3, axis[1])):

            def src(slot, c, k=k):
                return self.acc.ref.at[c, k]

            def dst(c, k=k):
                return self.came.ref.at[c, k - 1]

            self.copies.append(Copy(pool, to, src, dst, steps, steps))


class Fan:
    def __init__(self, pool, steps, rows, cols):
        self.acc = Scratch(pool, pltpu.VMEM((steps, 8, rows, cols), jnp.float32))
        self.came = Scratch(pool, pltpu.VMEM((steps, 8, rows, cols), jnp.float32))
        self.copies = {}
        for at, to in ((1, YH), (2, XP), (3, XPH), (4, X2), (5, X2H), (6, XM), (7, XMH)):

            def src(slot, c, at=at):
                return self.acc.ref.at[c, at]

            def dst(c, at=at):
                return self.came.ref.at[c, at]

            self.copies[at] = Copy(pool, to, src, dst, steps, steps)


class Swap:
    def __init__(self, pool, to, steps, slots, shape):
        self.out = Scratch(pool, pltpu.VMEM((slots, *shape), jnp.float32))
        self.own = Scratch(pool, pltpu.VMEM((slots, *shape), jnp.float32))
        self.came = Scratch(pool, pltpu.VMEM((steps, *shape), jnp.float32))
        self.copy = Copy(
            pool, to, lambda slot, c: self.out.ref.at[slot], lambda c: self.came.ref.at[c], slots, steps
        )


class Side:
    def __init__(self, pool, to, steps, slots, shape):
        self.out = Scratch(pool, pltpu.VMEM((slots, *shape), jnp.float32))
        self.came = Scratch(pool, pltpu.VMEM((steps, *shape), jnp.float32))
        self.copy = Copy(
            pool, to, lambda slot, c: self.out.ref.at[slot], lambda c: self.came.ref.at[c], slots, steps
        )


class Steps:
    def __init__(self, pool, widths, steps, first_column, slots, grad_slots):
        self.widths, self.steps, self.first_column = widths, steps, first_column
        self.cols = sum(widths.values())
        self.start = {X: 0, Z: widths[X], Y: widths[X] + widths[Z]}
        self.slots, self.grad_slots = slots, grad_slots
        self.grad = Scratch(pool, pltpu.VMEM((grad_slots, 512, self.cols), jnp.bfloat16))
        self.grad_sem = Scratch(pool, pltpu.SemaphoreType.DMA((grad_slots,)))
        self.out_sem = Scratch(pool, pltpu.SemaphoreType.DMA((3, slots)))
        self.swap = {t: Swap(pool, YN, steps, slots, (16, widths[t])) for t in (X, Z)}
        self.side = Side(pool, YN, steps, slots, (4, 64, widths[Y]))
        self.core = Swap(pool, CORE, steps, slots, (32, self.cols))

    def columns(self, c, offset=0, width=None):
        return pl.ds(
            pl.multiple_of(self.first_column + c * self.cols + offset, 128), self.cols if width is None else width
        )


def plan():
    pool = []
    state = [Scratch(pool, pltpu.VMEM((16, D), jnp.float32)) for _ in range(3)]
    state_sem = Scratch(pool, pltpu.SemaphoreType.DMA((3,)))
    select = Scratch(pool, pltpu.VMEM((64, 16), jnp.float32))
    wide = Steps(pool, WIDE, WIDE_STEPS, 0, SLOTS, GRAD_SLOTS)
    n = WIDE_STEPS
    wide.level = {
        t: [
            Ring(pool, AXES[t][0], n, 32 if t == Y else 64, WIDE[t], t != Y),
            Ring(pool, AXES[t][1], n, 8 if t == Y else 16, WIDE[t], False),
        ]
        for t in (X, Z, Y)
    }
    wide.yh = Swap(pool, YH, n, SLOTS, (8, WIDE_COLS // 2))
    wide.parity = Ring(pool, AXES[X][0], n, 8, WIDE_COLS // 2, False)
    n = NARROW_STEPS
    narrow = Steps(pool, NARROW, n, WIDE_STEPS * WIDE_COLS, n, n)
    narrow.level = {
        t: [
            Direct(pool, AXES[t][0], n, 64 if t == Y else 128, NARROW[t]),
            Direct(pool, AXES[t][1], n, 16 if t == Y else 32, NARROW[t]),
        ]
        for t in (X, Z, Y)
    }
    narrow.parity = Fan(pool, n, 8, NARROW_COLS // 2)
    return pool, state, state_sem, select, wide, narrow


def kernel(planned, grads, master, one, two, generator, member_slot, holder, *rest):
    pool, state, state_sem, select, wide, narrow = planned
    outs, parity = rest[:3], rest[3]
    for made, ref in zip(pool, rest[4:], strict=True):
        made.ref = ref
    dp, code = lax.axis_index("dp"), lax.axis_index("code")
    x, yl, z = dp // 8, lax.rem(dp // 4, 2), lax.rem(dp, 4)
    yh, core = code // 2, lax.rem(code, 2)

    def device(x=x, yl=yl, z=z, yh=yh, core=core):
        return (x * 8 + yl * 4 + z, yh * 2 + core)

    def around(at, by):
        return lax.rem(at + by, 4)

    where = {
        XP: device(x=around(x, 1)),
        XM: device(x=around(x, 3)),
        X2: device(x=around(x, 2)),
        ZP: device(z=around(z, 1)),
        ZM: device(z=around(z, 3)),
        Z2: device(z=around(z, 2)),
        YN: device(yl=1 - yl),
        YH: device(yh=1 - yh),
        CORE: device(core=1 - core),
        XPH: device(x=around(x, 1), yh=1 - yh),
        XMH: device(x=around(x, 3), yh=1 - yh),
        X2H: device(x=around(x, 2), yh=1 - yh),
    }
    place = {X: (x, z), Z: (z, x), Y: (z, x)}

    def start(copy, c):
        copy.at(c, where).start()

    def arrive(*copies, c):
        for copy in copies:
            copy.at(c, where).wait_recv()

    def left(*copies, c):
        for copy in copies:
            copy.at(c, where).wait_send()

    def load(s, c):
        slot = lax.rem(c, s.grad_slots)
        return pltpu.make_async_copy(
            grads.at[0, 0, :, s.columns(c)], s.grad.ref.at[slot], s.grad_sem.ref.at[slot]
        )

    given = [
        pltpu.make_async_copy(ref.at[0], held.ref, state_sem.ref.at[at])
        for at, (ref, held) in enumerate(zip((master, one, two), state, strict=True))
    ]

    def store(s, at, c):
        columns = s.columns(c)
        return pltpu.make_async_copy(
            state[at].ref.at[:, columns],
            outs[at].at[0, :, columns],
            s.out_sem.ref.at[at, lax.rem(c, s.slots)],
        )

    def grad(s, t, c, row, rows):
        block = s.grad.ref[
            lax.rem(c, s.grad_slots), pl.ds(pl.multiple_of(row, 16), rows), pl.ds(s.start[t], s.widths[t])
        ]
        return block.astype(jnp.float32)

    def first_row(t, a, h, b):
        return (a * 128 + b * 16 if t == X else a * 16 + b * 128) + h * 64

    def own(s, t, c, a, h):
        if t == X:
            return [(0, 64, grad(s, t, c, first_row(t, a, h, 0), 64))]
        return [(16 * b, 16, grad(s, t, c, first_row(t, a, h, b), 16)) for b in range(4)]

    def fill_side(s, c):
        slot = lax.rem(c, s.slots)
        for b in range(4):
            s.side.out.ref[slot, b] = grad(s, Y, c, b * 128 + (1 - yl) * 64, 64)

    def side_block(s, c, at, b):
        mine = grad(s, Y, c, b * 128 + yl * 64 + at * 16, 16)
        return mine + s.side.came.ref[c, b, pl.ds(pl.multiple_of(at * 16, 16), 16)]

    def adam(s, t, c, summed):
        columns = s.columns(c, s.start[t], s.widths[t])
        held_master, held_one, held_two = (held.ref for held in state)
        weights = held_master[:, columns]
        new_one = beta_one * held_one[:, columns] + (1.0 - beta_one) * summed
        new_two = beta_two * held_two[:, columns] + (1.0 - beta_two) * summed * summed
        direction = new_one / correct_one / (jnp.sqrt(new_two / correct_two) + epsilon)
        held_master[:, columns] = weights - learn_rate * (direction + decay_rate * weights)
        held_one[:, columns] = new_one
        held_two[:, columns] = new_two

    def terms(s, c):
        slot = lax.rem(c, s.slots)
        updated = state[0].ref[:, s.columns(c)]

        def weighted(rows):
            return jnp.dot(
                select.ref[rows], updated, precision=lax.Precision.HIGHEST, preferred_element_type=jnp.float32
            )

        s.core.out.ref[slot] = weighted(pl.ds(32, 32))
        start(s.core.copy, c)
        for at in range(3):
            store(s, at, c).start()
        s.core.own.ref[slot] = weighted(pl.ds(0, 32))

    def end_swaps(s, c, halves):
        slot = lax.rem(c, s.slots)
        for t in (X, Z):
            arrive(s.swap[t].copy, c=c)
            adam(s, t, c, s.swap[t].own.ref[slot] + s.swap[t].came.ref[c])
        adam(s, Y, c, halves)
        terms(s, c)

    def start_swap(s, t, c, low, high):
        slot = lax.rem(c, s.slots)
        s.swap[t].out.ref[slot] = jnp.where(yl == 0, high, low)
        start(s.swap[t].copy, c)
        s.swap[t].own.ref[slot] = jnp.where(yl == 0, low, high)

    def write_parity(s, c, total):
        half = s.cols // 2
        for h in range(2):
            parity[0, :, s.columns(c, half * h, half)] = total[4 * h : 4 * h + 4]


    def pass_on(ring, c, mine):
        for way in range(2):
            arrive(ring.copies[way], c=c)
            for row, rows, value in mine(way):
                ring.came[way].ref[c, 0, pl.ds(row, rows)] += value
            start(ring.on[way], c)

    def held_part(ring, c):
        slot = lax.rem(c, SLOTS)
        rows = ring.acc.spec.shape[2]
        return lambda way: [(0, rows, ring.acc.ref[slot, 4 + way])]

    def grad_part(t, c):
        a = place[t][0]
        return lambda way: own(wide, t, c, around(a, (1, 3)[way]), way)

    def fill_eight(ring, c, block):
        slot = lax.rem(c, SLOTS)

        def put(k, h):
            ring.acc.ref[slot, PLACE[k, h]] = block(k, h)

        put(2, 0)
        put(1, 1)
        start(ring.copies[0], c)
        put(2, 1)
        put(3, 0)
        start(ring.copies[1], c)
        for k, h in ((1, 0), (3, 1), (0, 0), (0, 1)):
            put(k, h)

    def halves(ring, c):
        slot = lax.rem(c, SLOTS)
        arrive(*ring.on, c=c)
        return [
            ring.acc.ref[slot, 6 + h] + ring.came[1 - h].ref[c, 1] + ring.passed.ref[c, h] for h in range(2)
        ]

    def second_axis(t, c):
        slot = lax.rem(c, SLOTS)
        ring, after = wide.level[t]
        r = after.acc.spec.shape[2]
        at_a, at_b = place[t]
        arrive(*ring.on, c=c)

        def block(k, h):
            b = around(at_b, k)
            rows = pl.ds(pl.multiple_of(b * r, r), r)
            if t == Y:
                mine = ring.acc.ref[slot, 6 + h, rows]
            else:
                mine = grad(wide, t, c, first_row(t, at_a, h, b), 16)
            return mine + ring.came[1 - h].ref[c, 1, rows] + ring.passed.ref[c, h, rows]

        fill_eight(after, c, block)

    def fill_wide(c):
        slot = lax.rem(c, SLOTS)
        load(wide, c).wait()
        fill_side(wide, c)
        for t in (X, Z):
            ring, a = wide.level[t][0], place[t][0]
            for way, parts in enumerate((((2, 0), (1, 1)), ((2, 1), (3, 0)))):
                for at, (k, h) in enumerate(parts):
                    for row, rows, value in own(wide, t, c, around(a, k), h):
                        ring.staged[way].ref[slot, at, pl.ds(row, rows)] = value

    def wide0(c):
        start(wide.side.copy, c)
        for way in range(2):
            for t in (X, Z):
                start(wide.level[t][0].copies[way], c)

    def wide1(c):
        slot = lax.rem(c, SLOTS)
        for t in (X, Z):
            pass_on(wide.level[t][0], c, grad_part(t, c))
        arrive(wide.side.copy, c=c)
        ring = wide.level[Y][0]

        def block(k):
            at = around(z, k)
            for b in range(4):
                total = side_block(wide, c, at, b)
                for h in range(2):
                    ring.acc.ref[slot, PLACE[k, h], pl.ds(8 * b, 8)] = total[8 * h : 8 * h + 8]

        block(2)
        block(1)
        start(ring.copies[0], c)
        block(3)
        start(ring.copies[1], c)
        block(0)

    def wide2(c):
        left(*wide.level[X][0].copies, *wide.level[Z][0].copies, wide.side.copy, c=c)
        for t in (X, Z):
            second_axis(t, c)
        pass_on(wide.level[Y][0], c, held_part(wide.level[Y][0], c))

    def wide3(c):
        left(*wide.level[X][0].on, *wide.level[Z][0].on, *wide.level[Y][0].copies, c=c)
        for t in (X, Z):
            pass_on(wide.level[t][1], c, held_part(wide.level[t][1], c))
        second_axis(Y, c)

    def wide4(c):
        left(*wide.level[X][1].copies, *wide.level[Z][1].copies, *wide.level[Y][0].on, c=c)
        for t in (X, Z):
            start_swap(wide, t, c, *halves(wide.level[t][1], c))
        pass_on(wide.level[Y][1], c, held_part(wide.level[Y][1], c))

    def wide5(c):
        left(*wide.level[X][1].on, *wide.level[Z][1].on, *wide.level[Y][1].copies, c=c)

        @pl.when(c == 0)
        def _():
            for copy in given:
                copy.wait()

        end_swaps(wide, c, jnp.concatenate(halves(wide.level[Y][1], c), axis=0))

    def wide6(c):
        slot = lax.rem(c, SLOTS)
        left(wide.swap[X].copy, wide.swap[Z].copy, *wide.level[Y][1].on, c=c)
        arrive(wide.core.copy, c=c)
        half = WIDE_COLS // 2

        def block(k, h):
            rows, columns = pl.ds(8 * k, 8), pl.ds(half * h, half)
            return wide.core.own.ref[slot, rows, columns] + wide.core.came.ref[c, rows, columns]

        fill_eight(wide.parity, c, block)

    def wide7(c):
        left(wide.core.copy, c=c)
        pass_on(wide.parity, c, held_part(wide.parity, c))
        for at in range(3):
            store(wide, at, c).wait()

    def wide8(c):
        slot = lax.rem(c, SLOTS)
        left(*wide.parity.copies, c=c)
        low, high = halves(wide.parity, c)
        wide.yh.out.ref[slot] = jnp.concatenate([low[4:8], high[4:8]], axis=0)
        start(wide.yh.copy, c)
        wide.yh.own.ref[slot] = jnp.concatenate([low[0:4], high[0:4]], axis=0)

    def wide9(c):
        left(*wide.parity.on, c=c)
        arrive(wide.yh.copy, c=c)
        write_parity(wide, c, wide.yh.own.ref[lax.rem(c, SLOTS)] + wide.yh.came.ref[c])
        left(wide.yh.copy, c=c)


    def fill_four(level, c, block):
        for k in (2, 1, 3):
            block(k)
            start(level.copies[k - 1], c)
        block(0)

    def whole(level, c):
        arrive(*level.copies, c=c)
        acc, came = level.acc.ref, level.came.ref
        return (acc[c, 0] + came[c, 0]) + (came[c, 1] + came[c, 2])

    def fill_narrow(c):
        load(narrow, c).wait()
        fill_side(narrow, c)
        for t in (X, Z):
            for k in range(4):
                for h in range(2):
                    for row, rows, value in own(narrow, t, c, around(place[t][0], k), h):
                        narrow.level[t][0].acc.ref[c, k, pl.ds(64 * h + row, rows)] = value

    def narrow0(c):
        start(narrow.side.copy, c)
        for k in (2, 1, 3):
            for t in (X, Z):
                start(narrow.level[t][0].copies[k - 1], c)

    def narrow1(c):
        for t in (X, Z):
            level, after = narrow.level[t]
            arrive(*level.copies, c=c)

            def block(k, t=t, level=level, after=after):
                b = around(place[t][1], k)
                for h in range(2):
                    rows = pl.ds(pl.multiple_of(64 * h + 16 * b, 16), 16)
                    acc, came = level.acc.ref, level.came.ref
                    after.acc.ref[c, k, pl.ds(16 * h, 16)] = (acc[c, 0, rows] + came[c, 0, rows]) + (
                        came[c, 1, rows] + came[c, 2, rows]
                    )

            fill_four(after, c, block)
        arrive(narrow.side.copy, c=c)
        level = narrow.level[Y][0]

        def side(k):
            for b in range(4):
                level.acc.ref[c, k, pl.ds(16 * b, 16)] = side_block(narrow, c, around(z, k), b)

        fill_four(level, c, side)

    def narrow2(c):
        for t in (X, Z):
            both = whole(narrow.level[t][1], c)
            start_swap(narrow, t, c, both[0:16], both[16:32])
        level, after = narrow.level[Y]
        arrive(*level.copies, c=c)

        def block(k):
            rows = pl.ds(pl.multiple_of(16 * around(x, k), 16), 16)
            acc, came = level.acc.ref, level.came.ref
            after.acc.ref[c, k] = (acc[c, 0, rows] + came[c, 0, rows]) + (came[c, 1, rows] + came[c, 2, rows])

        fill_four(after, c, block)

    def narrow3(c):
        end_swaps(narrow, c, whole(narrow.level[Y][1], c))

    def narrow4(c):
        arrive(narrow.core.copy, c=c)
        fan, half = narrow.parity, NARROW_COLS // 2
        for k in (2, 1, 3, 0):
            rows = pl.ds(8 * k, 8)
            block = narrow.core.own.ref[c, rows] + narrow.core.came.ref[c, rows]
            for other in (1, 0):
                part = block[4 * other : 4 * other + 4]
                fan.acc.ref[c, 2 * k + other] = jnp.concatenate([part[:, 0:half], part[:, half:]], axis=0)
                if k or other:
                    start(fan.copies[2 * k + other], c)

    def narrow5(c):
        fan = narrow.parity
        arrive(*fan.copies.values(), c=c)
        total = fan.acc.ref[c, 0]
        for at in fan.copies:
            total += fan.came.ref[c, at]
        write_parity(narrow, c, total)
        for t in (X, Z):
            left(*narrow.level[t][0].copies, *narrow.level[t][1].copies, narrow.swap[t].copy, c=c)
        left(*narrow.level[Y][0].copies, *narrow.level[Y][1].copies, narrow.side.copy, c=c)
        left(narrow.core.copy, *fan.copies.values(), c=c)
        for at in range(3):
            store(narrow, at, c).wait()

    def selector():
        def iota(shape, dimension):
            return lax.broadcasted_iota(jnp.int32, shape, dimension)

        def parts(shape):
            row = iota(shape, 0)
            d = row // 4
            first = lax.rem(x + lax.rem(d // 2, 4), 4) * 8 + lax.rem(dp, 8)
            second = lax.rem(yh + lax.rem(d, 2), 2) * 2 + lax.rem(core + d // 8, 2)
            return first, second, lax.rem(row, 4).astype(jnp.float32)

        first, second, _ = parts((64, 32))
        held = holder[...].astype(jnp.float32)
        mask = first == iota((64, 32), 1)
        picked = jnp.zeros((64, 32), jnp.float32)
        for at in range(4):
            picked += jnp.where(mask & (second == at), held[at : at + 1, :], 0.0)
        block = jnp.sum(picked, axis=1, keepdims=True)
        lane = iota((64, 16), 1)
        lane_value = lane.astype(jnp.float32)
        hit = lane_value == block
        column = jnp.sum(
            jnp.where(iota((4, 16), 1) == member_slot[...], generator[...], 0.0), axis=1, keepdims=True
        )
        spread = jnp.sum(jnp.where(iota((4, 16), 0) == iota((4, 16), 1) // 4, column, 0.0), axis=0, keepdims=True)
        scale = jnp.sum(jnp.where(hit, spread, 0.0), axis=1, keepdims=True)
        quarter = jnp.sum(
            jnp.where(hit, lax.rem(lane, 4).astype(jnp.float32), 0.0), axis=1, keepdims=True
        )
        _, _, row_in = parts((64, 16))
        select.ref[...] = jnp.where(lane_value == quarter * 4.0 + row_in, scale, 0.0)

    barrier = pltpu.get_barrier_semaphore()
    for to in where.values():
        pl.semaphore_signal(barrier, inc=1, device_id=to, device_id_type=MESH)
    for c in range(GRAD_SLOTS - 2):
        load(wide, c).start()
    for copy in given:
        copy.start()
    for c in range(NARROW_STEPS):
        load(narrow, c).start()
    fill_wide(0)
    selector()
    pl.semaphore_wait(barrier, len(where))

    wide_stages = (wide0, wide1, wide2, wide3, wide4, wide5, wide6, wide7, wide8, wide9)
    narrow_stages = (narrow0, narrow1, narrow2, narrow3, narrow4, narrow5)
    last = max(WIDE_STEPS + len(wide_stages), WIDE_STEPS + NARROW_STEPS + len(narrow_stages)) - 1

    def step(t, carry):
        for lag in range(len(wide_stages)):

            @pl.when((t >= lag) & (t < WIDE_STEPS + lag))
            def _(lag=lag):
                wide_stages[lag](t - lag)

            if lag < len(narrow_stages):
                begin = WIDE_STEPS + lag

                @pl.when((t >= begin) & (t < begin + NARROW_STEPS))
                def _(lag=lag, begin=begin):
                    narrow_stages[lag](t - begin)

        @pl.when(t + 1 < WIDE_STEPS)
        def _():
            fill_wide(t + 1)

        @pl.when((t + 1 >= WIDE_STEPS) & (t + 1 < WIDE_STEPS + NARROW_STEPS))
        def _():
            fill_narrow(t + 1 - WIDE_STEPS)

        @pl.when(t + GRAD_SLOTS - 2 < WIDE_STEPS)
        def _():
            load(wide, t + GRAD_SLOTS - 2).start()

        return carry

    lax.fori_loop(0, last, step, 0)


def finish(count, *refs):
    given, outs, held = refs[:count], refs[count : 2 * count], refs[2 * count : 3 * count]
    sem = refs[3 * count]
    parts = []
    for at in range(count):
        pieces = 4 if given[at].shape[1] % 16 == 0 else 1
        columns = given[at].shape[2] // pieces
        for piece in range(pieces):
            part = (slice(None), slice(None), pl.ds(piece * columns, columns))
            parts.append(
                (
                    pltpu.make_async_copy(given[at].at[part], held[at].at[part], sem.at[0, at, piece]),
                    pltpu.make_async_copy(held[at].at[part], outs[at].at[part], sem.at[1, at, piece]),
                )
            )
    for read, _ in parts:
        read.start()
    for read, write in parts:
        read.wait()
        write.start()
    for _, write in parts:
        write.wait()


def shards(grads, master, moment_one, moment_two, generator, member_slot, holder):
    planned = plan()
    anywhere = pl.BlockSpec(memory_space=pl.ANY)
    vmem = pl.BlockSpec(memory_space=pltpu.VMEM)
    state = jax.ShapeDtypeStruct(master.shape, jnp.float32)
    made = (state, state, state, jax.ShapeDtypeStruct((1, 4, D), jnp.float32))
    results = pl.pallas_call(
        functools.partial(kernel, planned),
        out_shape=made,
        in_specs=[anywhere] * 4 + [vmem] * 3,
        out_specs=(anywhere, anywhere, anywhere, vmem),
        scratch_shapes=[part.spec for part in planned[0]],
        name="adam_parity",
        compiler_params=pltpu.CompilerParams(
            collective_id=0, has_side_effects=True, vmem_limit_bytes=63 * 2**20
        ),
    )(grads, master, moment_one, moment_two, generator, member_slot, holder.T)
    return pl.pallas_call(
        functools.partial(finish, 4),
        out_shape=made,
        in_specs=[anywhere] * 4,
        out_specs=(anywhere,) * 4,
        scratch_shapes=[pltpu.VMEM(part.shape, part.dtype) for part in made] + [pltpu.SemaphoreType.DMA((2, 4, 4))],
        name="write_out",
        compiler_params=pltpu.CompilerParams(vmem_limit_bytes=63 * 2**20),
    )(*results)


def solution(mesh):
    state = P("code", "dp", None)
    return jax.shard_map(
        shards,
        mesh=mesh,
        in_specs=(P("dp", "code", None, None), state, state, state, P(), P("dp", "code"), P()),
        out_specs=(state, state, state, state),
        check_vma=False,
    )
```

time: 530 us -> 195 us (0.37)
  waiting for transfers between devices: 473 us -> 0 us
  Pallas kernels: 0 us -> 194 us
  other arithmetic: 27.9 us -> 0 us
  between operations: 14.8 us -> 1.29 us
  matrix products: 6.47 us -> 0 us
    reduce_scatter x1 -> x0, waiting for transfers between devices: 365 us -> none  [shards(): lax.psum_scatter(grad_block, 'dp', scatter_dimension=2, tiled=True)[0, 0]]
    pallas_call x0 -> x2, Pallas kernels: none -> 194 us  [the longest x1 191 us: shards(): pl.pallas_call(functools.partial(kernel, planned), out_shape=made, in_spe...]
    unnamed x3 -> x0, waiting for transfers between devices: 89 us -> none
    ppermute x2 -> x0, waiting for transfers between devices: 19.1 us -> none  [swapped(): return lax.ppermute(value, axis, pairs)]
    convert_element_type x2 -> x0, other arithmetic: 18.2 us -> none  [the longest x1 18.2 us: shards(): grad_block = grads.astype(jnp.float32)]
    dot_general x1 -> x0, matrix products: 6.47 us -> none  [shards(): jnp.einsum('qk,krd->qrd', selector, quarters, precision=lax.Precision.HIG...]
  transfers between devices with their start and end apart: 4 -> 0, of which waited for: 4 -> 0; matrix products, arithmetic and copies ran while one was open for 0% -> 0% of each run, Pallas kernels for 0% -> 0%
where the time goes in v1:
time: 195 us
  Pallas kernels  194 us (99%)
    pallas_call x1, Pallas kernels, shards(): pl.pallas_call(functools.partial(kernel, planned), out_shape=made, in_spe...  191 us

profile of v1, /device:TPU:0, one launch (start us, length us, event | category | flops | bytes accessed | tf_op | source)
XLA Modules:
  0.0 195.2 jit_solution(15240311093858078185)
XLA Ops:
  1.3 190.9 %adam_parity.1 = (f32[1,16,16384]{2,1,0:T(8,128)}, f32[1,16,16384]{2,1,0:T(8,128)}, f32[1,16,16384]{2,1,0:T(8,128)}, f32[1,4,16384]{2,1,0:T(4,128)}) custom-call(bf16[1,1,512,16384]{3,2,1,0:T(8,128)(2,1)} %grads.1, f32[1,16,16384]{2,1,0:T(8,128)} %master.1, f32[1,16,16384]{2,1,0:T(8,128)} %one.1, f32[1,16,16384]{2,1,0:T(8,128)} %two.1, f32[4,16]{1,0:T(4,128)} %generator.1, ...), custom_call_target="tpu_custom_call" | custom-call | tf_op jit(solution)/shard_map/adam_parity/pallas_call | solution.py:674
  192.2 3.0 %write_out.1 = (f32[1,16,16384]{2,1,0:T(8,128)}, f32[1,16,16384]{2,1,0:T(8,128)}, f32[1,16,16384]{2,1,0:T(8,128)}, f32[1,4,16384]{2,1,0:T(4,128)}) custom-call(f32[1,16,16384]{2,1,0:T(8,128)} %get-tuple-element.8.refs_0_, f32[1,16,16384]{2,1,0:T(8,128)} %get-tuple-element.9.refs_1_, f32[1,16,16384]{2,1,0:T(8,128)} %get-tuple-element.10.refs_2_, ...), custom_call_target="tpu_custom_call" | custom-call | tf_op jit(solution)/shard_map/write_out/pallas_call | solution.py:685

commit v2 on v1

--- a/solution.py
+++ b/solution.py
@@ -22,9 +22,9 @@
 XP, XM, X2, ZP, ZM, Z2, YN, YH, CORE, XPH, XMH, X2H = range(12)
 AXES = {X: ((XP, XM, X2), (ZP, ZM, Z2)), Z: ((ZP, ZM, Z2), (XP, XM, X2)), Y: ((ZP, ZM, Z2), (XP, XM, X2))}
 WIDE = {X: 384, Z: 256, Y: 384}
-WIDE_STEPS = 14
+WIDE_STEPS = 15
 NARROW = {X: 128, Z: 128, Y: 256}
-NARROW_STEPS = 4
+NARROW_STEPS = 2
 WIDE_COLS, NARROW_COLS = sum(WIDE.values()), sum(NARROW.values())
 GRAD_SLOTS = 5
 SLOTS = 3
@@ -85,19 +85,20 @@
 
 
 class Direct:
-    def __init__(self, pool, axis, steps, rows, cols):
-        self.acc = Scratch(pool, pltpu.VMEM((steps, 4, rows, cols), jnp.float32))
+    def __init__(self, pool, axis, steps, rows, cols, slots=None):
+        slots = slots or steps
+        self.acc = Scratch(pool, pltpu.VMEM((slots, 4, rows, cols), jnp.float32))
         self.came = Scratch(pool, pltpu.VMEM((steps, 3, rows, cols), jnp.float32))
-        self.copies = []
+        self.slots, self.copies = slots, []
         for k, to in ((1, axis[0]), (2, axis[2]), (3, axis[1])):
 
             def src(slot, c, k=k):
-                return self.acc.ref.at[c, k]
+                return self.acc.ref.at[slot, k]
 
             def dst(c, k=k):
                 return self.came.ref.at[c, k - 1]
 
-            self.copies.append(Copy(pool, to, src, dst, steps, steps))
+            self.copies.append(Copy(pool, to, src, dst, slots, steps))
 
 
 class Fan:
@@ -169,7 +170,8 @@
         for t in (X, Z, Y)
     }
     wide.yh = Swap(pool, YH, n, SLOTS, (8, WIDE_COLS // 2))
-    wide.parity = Ring(pool, AXES[X][0], n, 8, WIDE_COLS // 2, False)
+    wide.parity = Direct(pool, AXES[X][0], n, 8, WIDE_COLS, SLOTS)
+    wide.fan = Fan(pool, 1, 8, WIDE_COLS // 2)
     n = NARROW_STEPS
     narrow = Steps(pool, NARROW, n, WIDE_STEPS * WIDE_COLS, n, n)
     narrow.level = {
@@ -179,7 +181,7 @@
         ]
         for t in (X, Z, Y)
     }
-    narrow.parity = Fan(pool, n, 8, NARROW_COLS // 2)
+    narrow.fan = Fan(pool, n, 8, NARROW_COLS // 2)
     return pool, state, state_sem, select, wide, narrow
 
 
@@ -312,6 +314,29 @@
         for h in range(2):
             parity[0, :, s.columns(c, half * h, half)] = total[4 * h : 4 * h + 4]
 
+    def both_cores(s, c, k):
+        rows = pl.ds(8 * k, 8)
+        return s.core.own.ref[lax.rem(c, s.slots), rows] + s.core.came.ref[c, rows]
+
+    def fill_fan(s, c, at):
+        fan, half = s.fan, s.cols // 2
+        for k in (2, 1, 3, 0):
+            block = both_cores(s, c, k)
+            for other in (1, 0):
+                part = block[4 * other : 4 * other + 4]
+                fan.acc.ref[at, 2 * k + other] = jnp.concatenate([part[:, 0:half], part[:, half:]], axis=0)
+                if k or other:
+                    start(fan.copies[2 * k + other], at)
+
+    def end_fan(s, c, at):
+        fan = s.fan
+        arrive(*fan.copies.values(), c=at)
+        total = fan.acc.ref[at, 0]
+        for part in fan.copies:
+            total += fan.came.ref[at, part]
+        write_parity(s, c, total)
+        left(*fan.copies.values(), c=at)
+
 
     def pass_on(ring, c, mine):
         for way in range(2):
@@ -436,36 +461,44 @@
         end_swaps(wide, c, jnp.concatenate(halves(wide.level[Y][1], c), axis=0))
 
     def wide6(c):
-        slot = lax.rem(c, SLOTS)
-        left(wide.swap[X].copy, wide.swap[Z].copy, *wide.level[Y][1].on, c=c)
         arrive(wide.core.copy, c=c)
-        half = WIDE_COLS // 2
-
-        def block(k, h):
-            rows, columns = pl.ds(8 * k, 8), pl.ds(half * h, half)
-            return wide.core.own.ref[slot, rows, columns] + wide.core.came.ref[c, rows, columns]
-
-        fill_eight(wide.parity, c, block)
-
-    def wide7(c):
-        left(wide.core.copy, c=c)
-        pass_on(wide.parity, c, held_part(wide.parity, c))
+
+        @pl.when(c < WIDE_STEPS - 1)
+        def _():
+            slot = lax.rem(c, SLOTS)
+
+            def block(k):
+                wide.parity.acc.ref[slot, k] = both_cores(wide, c, k)
+
+            fill_four(wide.parity, c, block)
+
+        @pl.when(c == WIDE_STEPS - 1)
+        def _():
+            fill_fan(wide, c, 0)
+
+    def settle(c):
+        left(wide.swap[X].copy, wide.swap[Z].copy, *wide.level[Y][1].on, wide.core.copy, c=c)
         for at in range(3):
             store(wide, at, c).wait()
 
-    def wide8(c):
-        slot = lax.rem(c, SLOTS)
-        left(*wide.parity.copies, c=c)
-        low, high = halves(wide.parity, c)
+    def wide7(c):
+        slot, half = lax.rem(c, SLOTS), WIDE_COLS // 2
+        total = whole(wide.parity, c)
+        low, high = total[:, 0:half], total[:, half:]
         wide.yh.out.ref[slot] = jnp.concatenate([low[4:8], high[4:8]], axis=0)
         start(wide.yh.copy, c)
         wide.yh.own.ref[slot] = jnp.concatenate([low[0:4], high[0:4]], axis=0)
-
-    def wide9(c):
-        left(*wide.parity.on, c=c)
+        settle(c)
+
+    def wide8(c):
+        left(*wide.parity.copies, c=c)
         arrive(wide.yh.copy, c=c)
         write_parity(wide, c, wide.yh.own.ref[lax.rem(c, SLOTS)] + wide.yh.came.ref[c])
         left(wide.yh.copy, c=c)
+
+    def wide_end(_):
+        end_fan(wide, WIDE_STEPS - 1, 0)
+        settle(WIDE_STEPS - 1)
 
 
     def fill_four(level, c, block):
@@ -477,7 +510,7 @@
     def whole(level, c):
         arrive(*level.copies, c=c)
         acc, came = level.acc.ref, level.came.ref
-        return (acc[c, 0] + came[c, 0]) + (came[c, 1] + came[c, 2])
+        return (acc[lax.rem(c, level.slots), 0] + came[c, 0]) + (came[c, 1] + came[c, 2])
 
     def fill_narrow(c):
         load(narrow, c).wait()
@@ -537,27 +570,14 @@
 
     def narrow4(c):
         arrive(narrow.core.copy, c=c)
-        fan, half = narrow.parity, NARROW_COLS // 2
-        for k in (2, 1, 3, 0):
-            rows = pl.ds(8 * k, 8)
-            block = narrow.core.own.ref[c, rows] + narrow.core.came.ref[c, rows]
-            for other in (1, 0):
-                part = block[4 * other : 4 * other + 4]
-                fan.acc.ref[c, 2 * k + other] = jnp.concatenate([part[:, 0:half], part[:, half:]], axis=0)
-                if k or other:
-                    start(fan.copies[2 * k + other], c)
+        fill_fan(narrow, c, c)
 
     def narrow5(c):
-        fan = narrow.parity
-        arrive(*fan.copies.values(), c=c)
-        total = fan.acc.ref[c, 0]
-        for at in fan.copies:
-            total += fan.came.ref[c, at]
-        write_parity(narrow, c, total)
+        end_fan(narrow, c, c)
         for t in (X, Z):
             left(*narrow.level[t][0].copies, *narrow.level[t][1].copies, narrow.swap[t].copy, c=c)
         left(*narrow.level[Y][0].copies, *narrow.level[Y][1].copies, narrow.side.copy, c=c)
-        left(narrow.core.copy, *fan.copies.values(), c=c)
+        left(narrow.core.copy, c=c)
         for at in range(3):
             store(narrow, at, c).wait()
 
@@ -593,52 +613,56 @@
         _, _, row_in = parts((64, 16))
         select.ref[...] = jnp.where(lane_value == quarter * 4.0 + row_in, scale, 0.0)
 
+    def load_rest():
+        for c in range(2, GRAD_SLOTS - 1):
+            load(wide, c).start()
+        for copy in given:
+            copy.start()
+        for c in range(NARROW_STEPS):
+            load(narrow, c).start()
+        selector()
+
+    load(wide, 0).start()
     barrier = pltpu.get_barrier_semaphore()
     for to in where.values():
         pl.semaphore_signal(barrier, inc=1, device_id=to, device_id_type=MESH)
-    for c in range(GRAD_SLOTS - 2):
-        load(wide, c).start()
-    for copy in given:
-        copy.start()
-    for c in range(NARROW_STEPS):
-        load(narrow, c).start()
     fill_wide(0)
-    selector()
+    load(wide, 1).start()
     pl.semaphore_wait(barrier, len(where))
 
-    wide_stages = (wide0, wide1, wide2, wide3, wide4, wide5, wide6, wide7, wide8, wide9)
-    narrow_stages = (narrow0, narrow1, narrow2, narrow3, narrow4, narrow5)
-    last = max(WIDE_STEPS + len(wide_stages), WIDE_STEPS + NARROW_STEPS + len(narrow_stages)) - 1
+    first, wide_last, last = WIDE_STEPS, WIDE_STEPS - 1, NARROW_STEPS - 1
+    turn = (
+        (wide0, 0, wide_last), (narrow0, first, first + last),
+        (wide1, 1, wide_last + 1), (narrow1, first + 1, first + 1 + last),
+        (wide2, 2, wide_last + 2), (narrow2, first + 2, first + 2 + last),
+        (wide3, 3, wide_last + 3), (narrow3, first + 3, first + 3 + last),
+        (wide4, 4, wide_last + 4), (wide5, 5, wide_last + 5),
+        (narrow4, first + 3, first + 3 + last), (wide7, 6, wide_last + 5),
+        (narrow5, first + 4, first + 4 + last), (wide8, 7, wide_last + 6),
+        (wide_end, wide_last + 6, wide_last + 6),
+        (fill_wide, -1, wide_last - 1), (fill_narrow, first - 1, first - 1 + last),
+        (wide6, 5, wide_last + 5),
+    )
+    turns = 1 + max(end for _, _, end in turn)
 
     def step(t, carry):
-        for lag in range(len(wide_stages)):
-
-            @pl.when((t >= lag) & (t < WIDE_STEPS + lag))
-            def _(lag=lag):
-                wide_stages[lag](t - lag)
-
-            if lag < len(narrow_stages):
-                begin = WIDE_STEPS + lag
-
-                @pl.when((t >= begin) & (t < begin + NARROW_STEPS))
-                def _(lag=lag, begin=begin):
-                    narrow_stages[lag](t - begin)
-
-        @pl.when(t + 1 < WIDE_STEPS)
+        for stage, begin, end in turn:
+
+            @pl.when((t >= begin) & (t <= end))
+            def _(stage=stage, begin=begin):
+                stage(t - begin)
+
+        @pl.when(t == 0)
         def _():
-            fill_wide(t + 1)
-
-        @pl.when((t + 1 >= WIDE_STEPS) & (t + 1 < WIDE_STEPS + NARROW_STEPS))
-        def _():
-            fill_narrow(t + 1 - WIDE_STEPS)
-
-        @pl.when(t + GRAD_SLOTS - 2 < WIDE_STEPS)
+            load_rest()
+
+        @pl.when((t > 0) & (t + GRAD_SLOTS - 2 < WIDE_STEPS))
         def _():
             load(wide, t + GRAD_SLOTS - 2).start()
 
         return carry
 
-    lax.fori_loop(0, last, step, 0)
+    lax.fori_loop(0, turns, step, 0)
 
 
 def finish(count, *refs):

time: 195 us -> 191 us (0.979)
  Pallas kernels: 194 us -> 189 us
    pallas_call x1, Pallas kernels: 191 us -> 186 us  [shards(): pl.pallas_call(functools.partial(kernel, planned), out_shape=made, in_spe...]
where the time goes in v2:
time: 191 us
  Pallas kernels  189 us (99%)
    pallas_call x1, Pallas kernels, shards(): pl.pallas_call(functools.partial(kernel, planned), out_shape=made, in_spe...  186 us

profile of v2, /device:TPU:0, one launch (start us, length us, event | category | flops | bytes accessed | tf_op | source)
XLA Modules:
  0.0 190.7 jit_solution(11713928915092721471)
XLA Ops:
  1.3 186.4 %adam_parity.1 = (f32[1,16,16384]{2,1,0:T(8,128)}, f32[1,16,16384]{2,1,0:T(8,128)}, f32[1,16,16384]{2,1,0:T(8,128)}, f32[1,4,16384]{2,1,0:T(4,128)}) custom-call(bf16[1,1,512,16384]{3,2,1,0:T(8,128)(2,1)} %grads.1, f32[1,16,16384]{2,1,0:T(8,128)} %master.1, f32[1,16,16384]{2,1,0:T(8,128)} %one.1, f32[1,16,16384]{2,1,0:T(8,128)} %two.1, f32[4,16]{1,0:T(4,128)} %generator.1, ...), custom_call_target="tpu_custom_call" | custom-call | tf_op jit(solution)/shard_map/adam_parity/pallas_call | solution.py:698
  187.7 3.0 %write_out.1 = (f32[1,16,16384]{2,1,0:T(8,128)}, f32[1,16,16384]{2,1,0:T(8,128)}, f32[1,16,16384]{2,1,0:T(8,128)}, f32[1,4,16384]{2,1,0:T(4,128)}) custom-call(f32[1,16,16384]{2,1,0:T(8,128)} %get-tuple-element.8.refs_0_, f32[1,16,16384]{2,1,0:T(8,128)} %get-tuple-element.9.refs_1_, f32[1,16,16384]{2,1,0:T(8,128)} %get-tuple-element.10.refs_2_, ...), custom_call_target="tpu_custom_call" | custom-call | tf_op jit(solution)/shard_map/write_out/pallas_call | solution.py:709

commit v3 on v2

--- a/solution.py
+++ b/solution.py
@@ -412,9 +412,11 @@
                 start(wide.level[t][0].copies[way], c)
 
     def wide1(c):
+        for t in (X, Z):
+            pass_on(wide.level[t][0], c, grad_part(t, c))
+
+    def wide1_side(c):
         slot = lax.rem(c, SLOTS)
-        for t in (X, Z):
-            pass_on(wide.level[t][0], c, grad_part(t, c))
         arrive(wide.side.copy, c=c)
         ring = wide.level[Y][0]
 
@@ -433,21 +435,27 @@
         block(0)
 
     def wide2(c):
+        for t in (X, Z):
+            second_axis(t, c)
+
+    def wide2_side(c):
         left(*wide.level[X][0].copies, *wide.level[Z][0].copies, wide.side.copy, c=c)
-        for t in (X, Z):
-            second_axis(t, c)
         pass_on(wide.level[Y][0], c, held_part(wide.level[Y][0], c))
 
     def wide3(c):
+        for t in (X, Z):
+            pass_on(wide.level[t][1], c, held_part(wide.level[t][1], c))
+
+    def wide3_side(c):
         left(*wide.level[X][0].on, *wide.level[Z][0].on, *wide.level[Y][0].copies, c=c)
-        for t in (X, Z):
-            pass_on(wide.level[t][1], c, held_part(wide.level[t][1], c))
         second_axis(Y, c)
 
     def wide4(c):
+        for t in (X, Z):
+            start_swap(wide, t, c, *halves(wide.level[t][1], c))
+
+    def wide4_side(c):
         left(*wide.level[X][1].copies, *wide.level[Z][1].copies, *wide.level[Y][0].on, c=c)
-        for t in (X, Z):
-            start_swap(wide, t, c, *halves(wide.level[t][1], c))
         pass_on(wide.level[Y][1], c, held_part(wide.level[Y][1], c))
 
     def wide5(c):
@@ -624,23 +632,36 @@
 
     load(wide, 0).start()
     barrier = pltpu.get_barrier_semaphore()
-    for to in where.values():
-        pl.semaphore_signal(barrier, inc=1, device_id=to, device_id_type=MESH)
+    near = (XP, XM, ZP, ZM, YN, YH, CORE)
+    for to in near:
+        pl.semaphore_signal(barrier, inc=1, device_id=where[to], device_id_type=MESH)
     fill_wide(0)
     load(wide, 1).start()
-    pl.semaphore_wait(barrier, len(where))
+    pl.semaphore_wait(barrier, len(near))
 
     first, wide_last, last = WIDE_STEPS, WIDE_STEPS - 1, NARROW_STEPS - 1
     turn = (
-        (wide0, 0, wide_last), (narrow0, first, first + last),
-        (wide1, 1, wide_last + 1), (narrow1, first + 1, first + 1 + last),
-        (wide2, 2, wide_last + 2), (narrow2, first + 2, first + 2 + last),
-        (wide3, 3, wide_last + 3), (narrow3, first + 3, first + 3 + last),
-        (wide4, 4, wide_last + 4), (wide5, 5, wide_last + 5),
-        (narrow4, first + 3, first + 3 + last), (wide7, 6, wide_last + 5),
-        (narrow5, first + 4, first + 4 + last), (wide8, 7, wide_last + 6),
+        (wide0, 0, wide_last),
+        (narrow0, first, first + last),
+        (wide1, 1, wide_last + 1),
+        (wide4, 4, wide_last + 4),
+        (wide3, 3, wide_last + 3),
+        (wide2, 2, wide_last + 2),
+        (wide1_side, 1, wide_last + 1),
+        (narrow1, first + 1, first + 1 + last),
+        (wide2_side, 2, wide_last + 2),
+        (narrow2, first + 2, first + 2 + last),
+        (wide3_side, 3, wide_last + 3),
+        (narrow3, first + 3, first + 3 + last),
+        (wide4_side, 4, wide_last + 4),
+        (wide5, 5, wide_last + 5),
+        (narrow4, first + 3, first + 3 + last),
+        (wide7, 6, wide_last + 5),
+        (narrow5, first + 4, first + 4 + last),
+        (wide8, 7, wide_last + 6),
         (wide_end, wide_last + 6, wide_last + 6),
-        (fill_wide, -1, wide_last - 1), (fill_narrow, first - 1, first - 1 + last),
+        (fill_wide, -1, wide_last - 1),
+        (fill_narrow, first - 1, first - 1 + last),
         (wide6, 5, wide_last + 5),
     )
     turns = 1 + max(end for _, _, end in turn)

time: 191 us -> 189 us (0.990)
  no operation moved by 1% of the time
where the time goes in v3:
time: 189 us
  Pallas kernels  188 us (99%)
    pallas_call x1, Pallas kernels, shards(): pl.pallas_call(functools.partial(kernel, planned), out_shape=made, in_spe...  185 us

profile of v3, /device:TPU:0, one launch (start us, length us, event | category | flops | bytes accessed | tf_op | source)
XLA Modules:
  0.0 188.9 jit_solution(4064031993158421229)
XLA Ops:
  1.3 184.6 %adam_parity.1 = (f32[1,16,16384]{2,1,0:T(8,128)}, f32[1,16,16384]{2,1,0:T(8,128)}, f32[1,16,16384]{2,1,0:T(8,128)}, f32[1,4,16384]{2,1,0:T(4,128)}) custom-call(bf16[1,1,512,16384]{3,2,1,0:T(8,128)(2,1)} %grads.1, f32[1,16,16384]{2,1,0:T(8,128)} %master.1, f32[1,16,16384]{2,1,0:T(8,128)} %one.1, f32[1,16,16384]{2,1,0:T(8,128)} %two.1, f32[4,16]{1,0:T(4,128)} %generator.1, ...), custom_call_target="tpu_custom_call" | custom-call | tf_op jit(solution)/shard_map/adam_parity/pallas_call | solution.py:719
  185.9 3.0 %write_out.1 = (f32[1,16,16384]{2,1,0:T(8,128)}, f32[1,16,16384]{2,1,0:T(8,128)}, f32[1,16,16384]{2,1,0:T(8,128)}, f32[1,4,16384]{2,1,0:T(4,128)}) custom-call(f32[1,16,16384]{2,1,0:T(8,128)} %get-tuple-element.8.refs_0_, f32[1,16,16384]{2,1,0:T(8,128)} %get-tuple-element.9.refs_1_, f32[1,16,16384]{2,1,0:T(8,128)} %get-tuple-element.10.refs_2_, ...), custom_call_target="tpu_custom_call" | custom-call | tf_op jit(solution)/shard_map/write_out/pallas_call | solution.py:730
